TPU v7x, 128 devices: a whole 4x4x4 slice. The times are simulated.
128 devices in a mesh: ctx: 16 (over x, z), ch: 8 (over y, core).
Axes of the slice: x: 4, y: 4, z: 4, core: 2. Of those that a mesh axis runs over, the one named last changes fastest.
Arguments:
- inner_gate: bfloat16 [8192, 2048], P('ctx', 'ch'), may hold values from -6 to 6
- outer_gate: bfloat16 [8192, 2048], P('ctx', 'ch'), may hold values from -6 to 6
- source_values: bfloat16 [8192, 2048], P('ctx', 'ch'), may hold values from -6 to 6
- filter_taps: float32 [8192, 2048], P('ctx', 'ch'), may hold values from -1.1 to 1.1, as said below
- skip_gain: float32 [2048], P('ch'), may hold values from -1 to 1
- output_weight: bfloat16 [2048, 2048], replicated, may hold values from -0.125 to 0.125
Outputs:
- projected: bfloat16 [8192, 2048], P('ctx', 'ch')
Inputs may be any that keep to these rules, and one draw needn't show every extreme that they name: `filter_taps`: filter taps for lags 0 to 8191 of each channel.
All inputs are finite; a program needn't handle non-finite values.
Results may differ from a plain program's by a relative error of at most 0.0049.
Values may be sent and summed in bfloat16 or wider, within the bound.
A program may use at most 128 MiB of HBM per device.

v0:
```python
import math

import jax
import jax.numpy as jnp
from jax import lax
from jax.sharding import PartitionSpec as P

precise = lax.Precision.HIGHEST


def partner_2(value, axis, bit):
    mask = 2**bit
    pairs = [(source, source ^ mask) for source in range(lax.axis_size(axis))]
    return lax.ppermute(value, axis, pairs)


def split_length(length):
    smaller = 1
    for factor in range(1, math.isqrt(length) + 1):
        if length % factor == 0:
            smaller = factor
    return (smaller, length // smaller)


def twiddle_table(rows_count, cols_count, length, orient):
    row_index = jnp.arange(rows_count, dtype=jnp.int32)
    col_index = jnp.arange(cols_count, dtype=jnp.int32)
    product = row_index[:, None] * col_index[None, :] % length
    radians = orient * 2.0 * math.pi / length * product.astype(jnp.float32)
    return (jnp.cos(radians), jnp.sin(radians))


def fourier_table(length, orient):
    return twiddle_table(length, length, length, orient)


def complex_apply(table_real, table_imag, packed, pattern):
    half_width = packed.shape[-1] // 2
    direct = jnp.einsum(pattern, table_real, packed, precision=precise)
    crossed = jnp.einsum(pattern, table_imag, packed, precision=precise)
    return direct + jnp.concatenate(
        [-crossed[..., half_width:], crossed[..., :half_width]], axis=-1
    )


def rotate(packed, cosine_part, sine_part):
    half_width = packed.shape[-1] // 2
    real_part = packed[..., :half_width]
    imag_part = packed[..., half_width:]
    return jnp.concatenate(
        [
            real_part * cosine_part - imag_part * sine_part,
            real_part * sine_part + imag_part * cosine_part,
        ],
        axis=-1,
    )


def local_forward(packed):
    groups, length, double = packed.shape
    smaller, larger = split_length(length)
    blocks = packed.reshape(groups, larger, smaller, double)
    outer_real, outer_imag = fourier_table(larger, -1.0)
    sectioned = complex_apply(outer_real, outer_imag, blocks, "kb,gbac->gkac")
    cosine_part, sine_part = twiddle_table(larger, smaller, length, -1.0)
    sectioned = rotate(sectioned, cosine_part[None, :, :, None], sine_part[None, :, :, None])
    inner_real, inner_imag = fourier_table(smaller, -1.0)
    sectioned = complex_apply(inner_real, inner_imag, sectioned, "ja,gkac->gkjc")
    return sectioned.reshape(groups, length, double)


def local_inverse(packed):
    groups, length, double = packed.shape
    smaller, larger = split_length(length)
    blocks = packed.reshape(groups, larger, smaller, double)
    inner_real, inner_imag = fourier_table(smaller, 1.0)
    sectioned = complex_apply(inner_real, inner_imag, blocks, "ja,gkac->gkjc")
    cosine_part, sine_part = twiddle_table(larger, smaller, length, 1.0)
    sectioned = rotate(sectioned, cosine_part[None, :, :, None], sine_part[None, :, :, None])
    outer_real, outer_imag = fourier_table(larger, 1.0)
    sectioned = complex_apply(outer_real, outer_imag, sectioned, "kb,gbac->gkac")
    return sectioned.reshape(groups, length, double)


def spectral_product(packed):
    quarter = packed.shape[-1] // 4
    signal_real = packed[..., :quarter]
    kernel_real = packed[..., quarter : 2 * quarter]
    signal_imag = packed[..., 2 * quarter : 3 * quarter]
    kernel_imag = packed[..., 3 * quarter :]
    return jnp.concatenate(
        [
            signal_real * kernel_real - signal_imag * kernel_imag,
            signal_real * kernel_imag + signal_imag * kernel_real,
        ],
        axis=-1,
    )


def level_factors(position, level_bit, tok_count, orient):
    stride = 1 << level_bit
    upper_bit = position // stride % 2
    offset = position % stride * tok_count + jnp.arange(tok_count, dtype=jnp.int32)
    length = 2 * stride * tok_count
    radians = orient * 2.0 * math.pi / length * (offset * upper_bit).astype(jnp.float32)
    factor_sign = (1 - 2 * upper_bit).astype(jnp.float32)
    return (factor_sign, jnp.cos(radians)[:, None], jnp.sin(radians)[:, None])


def butterfly_convolve(signal, taps, position, ctx_count, padded_length):
    tok_count = signal.shape[0]
    levels = ctx_count.bit_length() - 1
    global_index = position * tok_count + jnp.arange(tok_count, dtype=jnp.int32)
    radians = -2.0 * math.pi / padded_length * global_index.astype(jnp.float32)
    cosine_part = jnp.cos(radians)[:, None]
    sine_part = jnp.sin(radians)[:, None]
    joined = jnp.concatenate([signal, taps], axis=-1)
    even_part = jnp.concatenate([joined, jnp.zeros_like(joined)], axis=-1)
    odd_part = jnp.concatenate([joined * cosine_part, joined * sine_part], axis=-1)
    current = jnp.stack([even_part, odd_part])
    for level_bit in reversed(range(levels)):
        factor_sign, level_cosine, level_sine = level_factors(position, level_bit, tok_count, -1.0)
        partner = partner_2(current, "ctx", level_bit)
        current = rotate(partner + factor_sign * current, level_cosine, level_sine)
    spectrum = local_forward(current)
    current = local_inverse(spectral_product(spectrum))
    for level_bit in range(levels):
        factor_sign, level_cosine, level_sine = level_factors(position, level_bit, tok_count, 1.0)
        turned = rotate(current, level_cosine, level_sine)
        partner = partner_2(turned, "ctx", level_bit)
        current = partner + factor_sign * turned
    half_width = current.shape[-1] // 2
    combined = (
        current[0, :, :half_width]
        + current[1, :, :half_width] * cosine_part
        + current[1, :, half_width:] * sine_part
    )
    return combined / padded_length


def on_device(inner_gate, outer_gate, source_values, filter_taps, skip_gain, output_weight):
    ctx_count = lax.axis_size("ctx")
    position = lax.axis_index("ctx")
    tok_count, channels = source_values.shape
    padded_length = 2 * ctx_count * tok_count
    signal = inner_gate.astype(jnp.float32) * source_values.astype(jnp.float32)
    convolved = butterfly_convolve(signal, filter_taps, position, ctx_count, padded_length)
    gated_rows = (
        outer_gate.astype(jnp.float32) * (convolved + skip_gain[None, :] * signal)
    ).astype(jnp.bfloat16)
    channel_rank = lax.axis_index("ch")
    weight_rows = lax.dynamic_slice_in_dim(output_weight, channel_rank * channels, channels, 0)
    projected = lax.psum_scatter(
        lax.dot_general(
            weight_rows, gated_rows, (((0,), (1,)), ((), ())), preferred_element_type=jnp.float32
        ),
        "ch",
        scatter_dimension=0,
        tiled=True,
    ).T
    return projected.astype(jnp.bfloat16)


def solution(mesh):
    in_specs = (P("ctx", "ch"), P("ctx", "ch"), P("ctx", "ch"), P("ctx", "ch"), P("ch"), P())
    out_specs = P("ctx", "ch")
    return jax.shard_map(
        on_device, mesh=mesh, in_specs=in_specs, out_specs=out_specs, check_vma=False
    )
```

profile of v0, /device:TPU:1, one launch (start us, length us, event | category | flops | bytes accessed | tf_op | source)
XLA Modules:
  0.0 691.0 jit_solution(2172444596231241976)
XLA Ops:
  6.6 1.1 convert_multiply_fusion
  7.8 1.3 maximum_bitcast_fusion
  9.4 2.5 pad_maximum_fusion
  12.1 3.6 collective-permute-start
  15.7 90.1 %collective-permute-done = f32[2,512,1024]{2,1,0:T(8,128)} collective-permute-done((f32[2,512,1024]{2,1,0:T(8,128)}, f32[2,512,1024]{2,1,0:T(8,128)}, u32[]{:S(2)}, u32[]{:S(2)}) %collective-permute-start) | collective-permute-done | bytes 4194336 | tf_op jit(solution)/shard_map/ppermute | solution.py:14
  105.8 3.8 multiply_add_fusion.3
  109.6 0.5 multiply_subtract_fusion.4
  110.2 2.6 pad_maximum_fusion.1
  112.8 1.6 collective-permute-start.1
  114.5 89.3 %collective-permute-done.1 = f32[2,512,1024]{2,1,0:T(8,128)} collective-permute-done((f32[2,512,1024]{2,1,0:T(8,128)}, f32[2,512,1024]{2,1,0:T(8,128)}, u32[]{:S(2)}, u32[]{:S(2)}) %collective-permute-start.1) | collective-permute-done | bytes 4194336 | tf_op jit(solution)/shard_map/ppermute | solution.py:14
  203.8 4.2 multiply_add_fusion.2
  207.9 0.5 multiply_subtract_fusion.3
  208.5 2.6 pad_maximum_fusion.2
  211.1 3.9 collective-permute-start.2
  215.1 88.7 %collective-permute-done.2 = f32[2,512,1024]{2,1,0:T(8,128)} collective-permute-done((f32[2,512,1024]{2,1,0:T(8,128)}, f32[2,512,1024]{2,1,0:T(8,128)}, u32[]{:S(2)}, u32[]{:S(2)}) %collective-permute-start.2) | collective-permute-done | bytes 4194336 | tf_op jit(solution)/shard_map/ppermute | solution.py:14
  303.7 4.2 multiply_add_fusion.1
  307.9 0.5 multiply_subtract_fusion.2
  308.5 2.6 pad_maximum_fusion.3
  311.1 0.9 collective-permute-start.3
  312.4 88.1 %collective-permute-done.3 = f32[2,512,1024]{2,1,0:T(8,128)} collective-permute-done((f32[2,512,1024]{2,1,0:T(8,128)}, f32[2,512,1024]{2,1,0:T(8,128)}, u32[]{:S(2)}, u32[]{:S(2)}) %collective-permute-start.3) | collective-permute-done | bytes 4194336 | tf_op jit(solution)/shard_map/ppermute | solution.py:14
  400.5 4.2 multiply_add_fusion
  404.7 0.5 multiply_subtract_fusion.1
  405.7 8.0 %fusion.10 = f32[2,32,16,1024]{3,1,2,0:T(8,128)S(1)} fusion(f32[2,32,16,1024]{3,2,1,0:T(8,128)S(1)} %bitcast.97), kind=kOutput, calls=%fused_computation.20 | convolution fusion | flops 402667520 | bytes 8388608 | tf_op jit(solution)/shard_map/kb,gbac->gkac/dot_general | solution.py:40
  413.7 0.5 slice_negate_fusion.1
  414.2 8.5 %maximum_add_fusion = f32[2,32,16,1024]{3,1,2,0:T(8,128)S(1)} fusion(f32[2,32,16,512]{3,1,2,0:T(8,128)S(1)} %get-tuple-element.20, f32[2,32,16,512]{3,1,2,0:T(8,128)S(1)} %get-tuple-element.19, f32[2,32,16,1024]{3,2,1,0:T(8,128)S(1)} %bitcast.98), kind=kOutput, calls=%fused_computation.5 | convolution fusion | flops 404764672 | bytes 12582912 | tf_op jit(solution)/shard_map/kb,gbac->gkac/dot_general | solution.py:39
  422.8 0.5 multiply_subtract_fusion
  423.8 7.7 %fusion.15 = f32[2,32,16,1024]{3,2,1,0:T(8,128)S(1)} fusion(f32[2,32,16,1024]{3,1,2,0:T(8,128)S(1)} %pad_maximum_fusion.5), kind=kOutput, calls=%fused_computation.21 | convolution fusion | flops 201330176 | bytes 8388608 | tf_op jit(solution)/shard_map/ja,gkac->gkjc/dot_general | solution.py:40
  431.5 0.9 slice_negate_fusion
  432.4 8.1 %maximum_add_fusion.1 = f32[2,32,16,1024]{3,2,1,0:T(8,128)S(1)} fusion(f32[2,32,16,512]{3,2,1,0:T(8,128)S(1)} %get-tuple-element.18, f32[2,32,16,512]{3,2,1,0:T(8,128)S(1)} %get-tuple-element.17, f32[2,32,16,1024]{3,1,2,0:T(8,128)S(1)} %pad_maximum_fusion.5), kind=kOutput, calls=%fused_computation.7 | convolution fusion | flops 203427328 | bytes 12582912 | tf_op jit(solution)/shard_map/ja,gkac->gkjc/dot_general | solution.py:39
  441.1 2.1 convolution_bitcast_fusion
  443.4 2.2 maximum_add_fusion.2
  446.4 3.3 fusion.24
  449.9 3.4 maximum_add_fusion.3
  453.3 1.2 copy.22
  455.2 0.5 collective-permute-start.4
  455.7 42.6 %collective-permute-done.4 = f32[2,512,512]{2,1,0:T(8,128)S(1)} collective-permute-done((f32[2,512,512]{2,1,0:T(8,128)S(1)}, f32[2,512,512]{2,1,0:T(8,128)S(1)}, u32[]{:S(2)}, u32[]{:S(2)}) %collective-permute-start.4) | collective-permute-done | bytes 2097184 | tf_op jit(solution)/shard_map/ppermute | solution.py:14
  499.4 2.2 collective-permute-start.5
  501.6 44.5 %collective-permute-done.5 = f32[2,512,512]{2,1,0:T(8,128)S(1)} collective-permute-done((f32[2,512,512]{2,1,0:T(8,128)S(1)}, f32[2,512,512]{2,1,0:T(8,128)S(1)}, u32[]{:S(2)}, u32[]{:S(2)}) %collective-permute-start.5) | collective-permute-done | bytes 2097184 | tf_op jit(solution)/shard_map/ppermute | solution.py:14
  547.2 1.5 collective-permute-start.6
  548.7 41.5 %collective-permute-done.6 = f32[2,512,512]{2,1,0:T(8,128)S(1)} collective-permute-done((f32[2,512,512]{2,1,0:T(8,128)S(1)}, f32[2,512,512]{2,1,0:T(8,128)S(1)}, u32[]{:S(2)}, u32[]{:S(2)}) %collective-permute-start.6) | collective-permute-done | bytes 2097184 | tf_op jit(solution)/shard_map/ppermute | solution.py:14
  591.0 1.7 pad_maximum_fusion.11
  592.6 2.7 collective-permute-start.7
  595.4 41.4 %collective-permute-done.7 = f32[2,512,512]{2,1,0:T(8,128)} collective-permute-done((f32[2,512,512]{2,1,0:T(8,128)}, f32[2,512,512]{2,1,0:T(8,128)}, u32[]{:S(2)}, u32[]{:S(2)}) %collective-permute-start.7) | collective-permute-done | bytes 2097184 | tf_op jit(solution)/shard_map/ppermute | solution.py:14
  636.8 2.0 multiply_add_fusion.4
  638.8 4.2 fusion.27
  643.0 38.9 %reduce-scatter.2.cloned.1.call-done = f32[256,512]{1,0:T(8,128)} async-done(((f32[2048,512]{1,0:T(8,128)}), f32[256,512]{1,0:T(8,128)}) %reduce-scatter.2.cloned.1.call-update) | async-done | bytes 524304 | tf_op jit(solution)/shard_map/reduce_scatter | solution.py:153
  682.0 1.1 convert_bitcast_fusion
  683.0 0.8 copy.23
  (56 shorter events, 7.2 us)
Async XLA Ops:
  6.5 675.4 %reduce-scatter.2.cloned.1.call-start = ((), (), s32[]{:S(2)}) async-start(), calls=%async_computation.1 | async-start | bytes 4718592 | tf_op jit(solution)/shard_map/reduce_scatter | solution.py:153
  6.6 2.5 copy-start.4
  9.4 2.7 copy-start
  12.1 93.7 %collective-permute-start = (f32[2,512,1024]{2,1,0:T(8,128)}, f32[2,512,1024]{2,1,0:T(8,128)}, u32[]{:S(2)}, u32[]{:S(2)}) collective-permute-start(f32[2,512,1024]{2,1,0:T(8,128)} %pad_maximum_fusion), channel_id=1, source_target_pairs={{0,64},{8,72},{16,80},{24,88},{32,96},{40,104},{48,112},{56,120},{... | collective-permute-start | bytes 12582920 | tf_op jit(solution)/shard_map/ppermute | solution.py:14
  110.2 2.7 copy-start.2
  112.8 90.9 %collective-permute-start.1 = (f32[2,512,1024]{2,1,0:T(8,128)}, f32[2,512,1024]{2,1,0:T(8,128)}, u32[]{:S(2)}, u32[]{:S(2)}) collective-permute-start(f32[2,512,1024]{2,1,0:T(8,128)} %pad_maximum_fusion.1), channel_id=1, source_target_pairs={{0,32},{8,40},{16,48},{24,56},{32,0},{40,8},{48,16},{56,24},{64,96... | collective-permute-start | bytes 12582920 | tf_op jit(solution)/shard_map/ppermute | solution.py:14
  208.5 2.7 copy-start.1
  211.1 92.6 %collective-permute-start.2 = (f32[2,512,1024]{2,1,0:T(8,128)}, f32[2,512,1024]{2,1,0:T(8,128)}, u32[]{:S(2)}, u32[]{:S(2)}) collective-permute-start(f32[2,512,1024]{2,1,0:T(8,128)} %pad_maximum_fusion.2), channel_id=1, source_target_pairs={{0,16},{8,24},{16,0},{24,8},{32,48},{40,56},{48,32},{56,40},{64,80... | collective-permute-start | bytes 12582920 | tf_op jit(solution)/shard_map/ppermute | solution.py:14
  308.5 2.7 copy-start.3
  311.1 89.4 %collective-permute-start.3 = (f32[2,512,1024]{2,1,0:T(8,128)}, f32[2,512,1024]{2,1,0:T(8,128)}, u32[]{:S(2)}, u32[]{:S(2)}) collective-permute-start(f32[2,512,1024]{2,1,0:T(8,128)} %pad_maximum_fusion.3), channel_id=1, source_target_pairs={{0,8},{8,0},{16,24},{24,16},{32,40},{40,32},{48,56},{56,48},{64,72... | collective-permute-start | bytes 12582920 | tf_op jit(solution)/shard_map/ppermute | solution.py:14
  455.2 43.2 %collective-permute-start.4 = (f32[2,512,512]{2,1,0:T(8,128)S(1)}, f32[2,512,512]{2,1,0:T(8,128)S(1)}, u32[]{:S(2)}, u32[]{:S(2)}) collective-permute-start(f32[2,512,512]{2,1,0:T(8,128)S(1)} %pad_maximum_fusion.8), channel_id=1, source_target_pairs={{0,8},{8,0},{16,24},{24,16},{32,40},{40,32},{48,56},{56,48},{64,72... | collective-permute-start | bytes 6291464 | tf_op jit(solution)/shard_map/ppermute | solution.py:14
  499.4 46.7 %collective-permute-start.5 = (f32[2,512,512]{2,1,0:T(8,128)S(1)}, f32[2,512,512]{2,1,0:T(8,128)S(1)}, u32[]{:S(2)}, u32[]{:S(2)}) collective-permute-start(f32[2,512,512]{2,1,0:T(8,128)S(1)} %pad_maximum_fusion.9), channel_id=1, source_target_pairs={{0,16},{8,24},{16,0},{24,8},{32,48},{40,56},{48,32},{56,40},{64,80... | collective-permute-start | bytes 6291464 | tf_op jit(solution)/shard_map/ppermute | solution.py:14
  547.2 43.0 %collective-permute-start.6 = (f32[2,512,512]{2,1,0:T(8,128)S(1)}, f32[2,512,512]{2,1,0:T(8,128)S(1)}, u32[]{:S(2)}, u32[]{:S(2)}) collective-permute-start(f32[2,512,512]{2,1,0:T(8,128)S(1)} %pad_maximum_fusion.10), channel_id=1, source_target_pairs={{0,32},{8,40},{16,48},{24,56},{32,0},{40,8},{48,16},{56,24},{64,96... | collective-permute-start | bytes 6291464 | tf_op jit(solution)/shard_map/ppermute | solution.py:14
  592.6 44.1 %collective-permute-start.7 = (f32[2,512,512]{2,1,0:T(8,128)}, f32[2,512,512]{2,1,0:T(8,128)}, u32[]{:S(2)}, u32[]{:S(2)}) collective-permute-start(f32[2,512,512]{2,1,0:T(8,128)} %pad_maximum_fusion.11), channel_id=1, source_target_pairs={{0,64},{8,72},{16,80},{24,88},{32,96},{40,104},{48,112},{56,120},{... | collective-permute-start | bytes 6291464 | tf_op jit(solution)/shard_map/ppermute | solution.py:14
  595.4 43.4 %copy-start.5 = (bf16[512,256]{1,0:T(8,128)(2,1)S(1)}, bf16[512,256]{1,0:T(8,128)(2,1)}, u32[]{:S(2)}) copy-start(bf16[512,256]{1,0:T(8,128)(2,1)} %param.8) | copy-start | bytes 786436
  595.4 43.4 %copy-start.6 = (bf16[512,256]{1,0:T(8,128)(2,1)S(1)}, bf16[512,256]{1,0:T(8,128)(2,1)}, u32[]{:S(2)}) copy-start(bf16[512,256]{1,0:T(8,128)(2,1)} %param.6) | copy-start | bytes 786436
  595.4 43.4 %copy-start.7 = (bf16[512,256]{1,0:T(8,128)(2,1)S(1)}, bf16[512,256]{1,0:T(8,128)(2,1)}, u32[]{:S(2)}) copy-start(bf16[512,256]{1,0:T(8,128)(2,1)} %param.7) | copy-start | bytes 786436
  595.4 43.4 %copy-start.8 = (f32[256]{0:T(256)S(1)}, f32[256]{0:T(256)}, u32[]{:S(2)}) copy-start(f32[256]{0:T(256)} %param.10) | copy-start | bytes 3076
Sparse Core Ops, SparseCore 0:
  643.1 38.7 reduce-scatter.1
where the time goes:
time: 699 us; the launch traced here: 691 us
  waiting for transfers between devices  565 us (81%)
  matrix products  47.6 us (7%)
  other arithmetic  44.9 us (6%)
  starting transfers between devices  16.9 us (2%)
  between operations  14.1 us (2%)
    ppermute x8, waiting for transfers between devices, partner_2(): return lax.ppermute(value, axis, pairs)  526 us
    reduce_scatter x1, waiting for transfers between devices, on_device(): lax.psum_scatter(lax.dot_general(weight_rows, gated_rows, (((0,), (1,)),...  38.9 us
    dot_general x4, matrix products, complex_apply(): direct = jnp.einsum(pattern, table_real, packed, precision=precise)  22.3 us
    dot_general x4, matrix products, complex_apply(): crossed = jnp.einsum(pattern, table_imag, packed, precision=precise)  21.1 us
    ppermute x8, starting transfers between devices, partner_2(): return lax.ppermute(value, axis, pairs)  16.9 us
    add x4, other arithmetic, butterfly_convolve(): current = rotate(partner + factor_sign * current, level_cosine, level_sine)  16.3 us
  transfers between devices with their start and end apart: 9, of which 9 were waited for; matrix products, arithmetic and copies ran while one was open for 0% of the time, Pallas kernels for 0%

commit v1 on v0

v1 whole, which is shorter than its diff:
```python
import functools

import jax
import jax.numpy as jnp
import ml_dtypes
import numpy as np
from jax import lax
from jax.experimental import pallas as pl
from jax.experimental.pallas import tpu as pltpu
from jax.sharding import PartitionSpec as P

MESH = pl.DeviceIdType.MESH
F32 = jnp.float32
BF16 = jnp.bfloat16

CTX = 16
SIDE = 4
TOK = 512
CH = 256
LANES = 128
CHUNKS = 2
GROUP = 8
PHASES = 16
PER = TOK // PHASES
ROWS = CTX * PER
LENGTH = ROWS * PHASES
FEATURES = 256
HALF = TOK // 2
BLOCK = 128


def split_table(table):
    high = table.astype(np.float32).astype(ml_dtypes.bfloat16)
    low = (table - high.astype(np.float64)).astype(np.float32).astype(ml_dtypes.bfloat16)
    return np.stack([high, low])


def tables():
    k_row = np.arange(ROWS) + 0.25
    rows = np.arange(ROWS)
    turn = 2.0 * np.pi * np.outer(k_row, rows) / ROWS
    row_forward = np.concatenate([np.cos(turn), -np.sin(turn)], axis=0)
    row_inverse = np.concatenate([np.cos(turn.T), -np.sin(turn.T)], axis=1)
    phase = np.repeat(np.arange(PHASES), GROUP)
    twist = 2.0 * np.pi * np.outer(k_row, phase) / LENGTH
    twiddle = np.stack([np.cos(twist), -np.sin(twist)]).astype(np.float32)
    untwiddle = (np.stack([np.cos(twist), np.sin(twist)]) / LENGTH).astype(np.float32)
    angle = 2.0 * np.pi * np.outer(np.arange(PHASES), np.arange(PHASES)) / PHASES
    cosine = np.kron(np.cos(angle), np.eye(GROUP))
    sine = np.kron(np.sin(angle), np.eye(GROUP))
    phase_forward = np.block([[cosine, -sine], [sine, cosine]])
    phase_inverse = np.block([[cosine, sine], [-sine, cosine]])
    return (
        split_table(row_forward),
        split_table(row_inverse),
        twiddle,
        untwiddle,
        split_table(phase_forward),
        split_table(phase_inverse),
    )


def swap_groups(parts, roll):
    parts = list(parts)
    lane = lax.broadcasted_iota(jnp.int32, parts[0].shape, 1)
    bit = PHASES // 2
    while bit:
        shift = bit * GROUP
        upper = (lane & shift) != 0
        for q in range(PHASES):
            if q & bit:
                continue
            first, second = parts[q], parts[q | bit]
            parts[q] = jnp.where(upper, roll(second, shift), first)
            parts[q | bit] = jnp.where(upper, second, roll(first, LANES - shift))
        bit //= 2
    return parts


def lane_roll(value, shift):
    return pltpu.roll(value, shift, 1)


def split(value):
    high = value.astype(BF16)
    return high, (value - high.astype(F32)).astype(BF16)


def dot(a, b):
    return jnp.dot(a, b, preferred_element_type=F32)


def dot3(value, table):
    high, low = split(value)
    return dot(high, table[0]) + dot(low, table[0]) + dot(high, table[1])


def kernel(
    inner, outer, source, taps, skip, weight, row_f, row_i, twid, untwid, ph_f, ph_i,
    out,
    v_inner, v_outer, v_source, v_taps, v_skip, v_weight, v_row_f, v_row_i, v_twid, v_untwid, v_ph_f, v_ph_i,
    signal, send, recv, spectrum, y_send, y_recv, y_full, gated, acc,
    load_sem, a_send, a_recv, b_send, b_recv, c_send, c_recv, s_send, s_recv,
):
    me = lax.axis_index("ctx")
    rank = lax.axis_index("ch")
    x_me, z_me = me // SIDE, me % SIDE
    y_me, core = rank // 2, rank % 2
    up = lax.rem(y_me + 1, SIDE) * 2 + core
    down = lax.rem(y_me + SIDE - 1, SIDE) * 2 + core
    sibling = y_me * 2 + (1 - core)

    def peer(k):
        return lax.rem(x_me + k // SIDE, SIDE) * SIDE + lax.rem(z_me + k % SIDE, SIDE)

    feature0 = pl.multiple_of(rank * FEATURES, FEATURES)
    loads = [
        pltpu.make_async_copy(src, dst, load_sem.at[n])
        for n, (src, dst) in enumerate(
            [
                (inner, v_inner),
                (source, v_source),
                (taps.at[:, :LANES], v_taps.at[0]),
                (taps.at[:, LANES:], v_taps.at[1]),
                (row_f, v_row_f),
                (twid, v_twid),
                (ph_f, v_ph_f),
                (ph_i, v_ph_i),
                (untwid, v_untwid),
                (row_i, v_row_i),
                (outer, v_outer),
                (skip, v_skip),
                (weight.at[:, pl.ds(feature0, FEATURES)], v_weight),
            ]
        )
    ]
    for load in loads:
        load.start()

    barrier = pltpu.get_barrier_semaphore()
    for k in range(1, CTX):
        pl.semaphore_signal(barrier, inc=1, device_id=(peer(k), rank), device_id_type=MESH)
    for other in (up, down, sibling):
        pl.semaphore_signal(barrier, inc=1, device_id=(me, other), device_id_type=MESH)

    for load in loads[:4]:
        load.wait()
    for chunk in range(CHUNKS):
        lanes = slice(chunk * LANES, (chunk + 1) * LANES)
        signal[chunk] = v_inner[:, lanes].astype(F32) * v_source[:, lanes].astype(F32)

    far_first = sorted(range(1, CTX), key=lambda k: -(2 - abs(2 - k // SIDE)) - (2 - abs(2 - k % SIDE)))

    def a_copy(chunk, k):
        to = peer(k)
        return pltpu.make_async_remote_copy(
            src_ref=send.at[chunk, to],
            dst_ref=recv.at[chunk, me],
            send_sem=a_send.at[chunk, k],
            recv_sem=a_recv.at[chunk, k],
            device_id=(to, rank),
            device_id_type=MESH,
        )

    for chunk in range(CHUNKS):
        for place, ref in enumerate((signal, v_taps)):
            parts = swap_groups([ref[chunk, pl.ds(q, PER, stride=PHASES), :] for q in range(PHASES)], lane_roll)
            for d in range(CTX):
                send[chunk, d, :, place * LANES : (place + 1) * LANES] = parts[d].astype(BF16)
        if chunk == 0:
            pl.semaphore_wait(barrier, CTX + 2)
        for k in far_first:
            a_copy(chunk, k).start()
        recv[chunk, me] = send[chunk, me]

    def b_copy(chunk, k):
        to = peer(k)
        return pltpu.make_async_remote_copy(
            src_ref=y_send.at[chunk, pl.ds(pl.multiple_of(to * PER, PER), PER)],
            dst_ref=y_recv.at[chunk, me],
            send_sem=b_send.at[chunk, k],
            recv_sem=b_recv.at[chunk, k],
            device_id=(to, rank),
            device_id_type=MESH,
        )

    def convolve(chunk):
        for k in range(1, CTX):
            a_copy(chunk, k).wait_recv()
        if chunk == 0:
            for load in loads[4:10]:
                load.wait()
        arrived = recv[chunk].reshape(ROWS, 2 * LANES)
        for start in range(0, ROWS, BLOCK):
            real_rows = pl.ds(start, BLOCK)
            imag_rows = pl.ds(ROWS + start, BLOCK)
            real = dot(v_row_f[0, real_rows], arrived) + dot(v_row_f[1, real_rows], arrived)
            imag = dot(v_row_f[0, imag_rows], arrived) + dot(v_row_f[1, imag_rows], arrived)
            cosine, sine = v_twid[0, real_rows], v_twid[1, real_rows]
            turned = []
            for place in (0, 1):
                re = real[:, place * LANES : (place + 1) * LANES]
                im = imag[:, place * LANES : (place + 1) * LANES]
                turned.append(jnp.concatenate([re * cosine - im * sine, re * sine + im * cosine], axis=1))
            both = dot3(jnp.concatenate(turned, axis=0), v_ph_f)
            xr, xi = both[:BLOCK, :LANES], both[:BLOCK, LANES:]
            hr, hi = both[BLOCK:, :LANES], both[BLOCK:, LANES:]
            product = jnp.concatenate([xr * hr - xi * hi, xr * hi + xi * hr], axis=1)
            back = dot3(product, v_ph_i)
            re, im = back[:, :LANES], back[:, LANES:]
            cosine, sine = v_untwid[0, real_rows], v_untwid[1, real_rows]
            for rows, value in (
                (real_rows, re * cosine - im * sine),
                (imag_rows, re * sine + im * cosine),
            ):
                high, low = split(value)
                spectrum[rows, :LANES] = high
                spectrum[rows, LANES:] = low
        for dx in (2, 1, 3, 0):
            to_x = lax.rem(x_me + dx, SIDE)
            rows = pl.ds(pl.multiple_of(to_x * BLOCK, BLOCK), BLOCK)
            wide = dot(v_row_i[0, rows], spectrum[...])
            y = wide[:, :LANES] + wide[:, LANES:] + dot(v_row_i[1, rows], spectrum[:, :LANES])
            y_send[chunk, rows] = y.astype(BF16)
            for dz in (2, 1, 3, 0):
                if dx or dz:
                    b_copy(chunk, dx * SIDE + dz).start()
        y_recv[chunk, me] = y_send[chunk, pl.ds(pl.multiple_of(me * PER, PER), PER)]

    def half(ref, h):
        return ref.at[pl.ds(h * HALF, HALF)]

    def ring_copy(chunk, frm, to_slot, h, device, sem):
        return pltpu.make_async_remote_copy(
            src_ref=half(gated.at[frm, 0, chunk], h),
            dst_ref=half(gated.at[to_slot, 0, chunk], h),
            send_sem=c_send.at[chunk, sem],
            recv_sem=c_recv.at[chunk, sem],
            device_id=(me, device),
            device_id_type=MESH,
        )

    def ring(chunk, name, h):
        if name == "up":
            return ring_copy(chunk, 0, 1, h, up, h)
        if name == "down":
            return ring_copy(chunk, 0, 3, h, down, 2 + h)
        return ring_copy(chunk, 1 if h == 0 else 3, 2, h, up if h == 0 else down, 4 + h)

    def pair_copy(chunk, slot, h):
        return pltpu.make_async_remote_copy(
            src_ref=half(gated.at[slot, 0, chunk], h),
            dst_ref=half(gated.at[slot, 1, chunk], h),
            send_sem=s_send.at[chunk, slot, h],
            recv_sem=s_recv.at[chunk, slot, h],
            device_id=(me, sibling),
            device_id_type=MESH,
        )

    def gate(chunk):
        for k in range(1, CTX):
            b_copy(chunk, k).wait_recv()
        if chunk == 0:
            for load in loads[10:]:
                load.wait()
        lanes = slice(chunk * LANES, (chunk + 1) * LANES)
        parts = swap_groups([y_recv[chunk, d].astype(F32) for d in range(CTX)], lane_roll)
        for q in range(PHASES):
            y_full[pl.ds(q, PER, stride=PHASES), :] = parts[q]
        for h in (0, 1):
            rows = slice(h * HALF, (h + 1) * HALF)
            total = y_full[rows, :] + v_skip[0:1, lanes] * signal[chunk, rows]
            gated[0, 0, chunk, rows] = (v_outer[rows, lanes].astype(F32) * total).astype(BF16)
            ring(chunk, "up", h).start()
            ring(chunk, "down", h).start()
            pair_copy(chunk, 0, h).start()

    def project(chunk, slot, h, first=False, last=False):
        y_from = lax.rem(y_me + SIDE - slot, SIDE)
        rows = slice(h * HALF, (h + 1) * HALF)
        left = jnp.concatenate([gated[slot, 0, chunk, rows], gated[slot, 1, chunk, rows]], axis=1)
        right = jnp.concatenate(
            [
                v_weight[pl.ds(pl.multiple_of((2 * y_from + c) * CH + chunk * LANES, LANES), LANES), :]
                for c in (core, 1 - core)
            ],
            axis=0,
        )
        term = dot(left, right)
        if not first:
            term = acc[rows] + term
        if last:
            out[rows] = term.astype(BF16)
        else:
            acc[rows] = term

    def near(chunk):
        for name, slot, h, far in (("up", 1, 0, True), ("down", 3, 1, True), ("up", 1, 1, False), ("down", 3, 0, False)):
            ring(chunk, name, h).wait_recv()
            if far:
                ring(chunk, "far", h).start()
            pair_copy(chunk, slot, h).start()

    def own(chunk):
        for h in (0, 1):
            pair_copy(chunk, 0, h).wait_recv()
            project(chunk, 0, h, first=chunk == 0)

    def finish(chunk):
        for slot, h in ((1, 0), (3, 1), (1, 1), (3, 0)):
            pair_copy(chunk, slot, h).wait_recv()
            project(chunk, slot, h)
        for h in (0, 1):
            ring(chunk, "far", h).wait_recv()
            pair_copy(chunk, 2, h).start()
        for h in (0, 1):
            pair_copy(chunk, 2, h).wait_recv()
            project(chunk, 2, h, last=chunk == CHUNKS - 1)

    convolve(0)
    convolve(1)
    gate(0)
    gate(1)
    near(0)
    own(0)
    near(1)
    own(1)
    finish(0)
    finish(1)

    for chunk in range(CHUNKS):
        for k in range(1, CTX):
            a_copy(chunk, k).wait_send()
            b_copy(chunk, k).wait_send()
        for name in ("up", "down", "far"):
            for h in (0, 1):
                ring(chunk, name, h).wait_send()
        for slot in range(SIDE):
            for h in (0, 1):
                pair_copy(chunk, slot, h).wait_send()


def on_device(inner_gate, outer_gate, source_values, filter_taps, skip_gain, output_weight):
    constants = [jnp.asarray(table) for table in tables()]
    operands = (inner_gate, outer_gate, source_values, filter_taps, skip_gain.reshape(1, CH), output_weight, *constants)
    vmem = pltpu.VMEM
    dma = pltpu.SemaphoreType.DMA
    return pl.pallas_call(
        kernel,
        out_shape=jax.ShapeDtypeStruct((TOK, FEATURES), BF16),
        in_specs=[pl.BlockSpec(memory_space=pl.ANY)] * len(operands),
        out_specs=pl.BlockSpec(memory_space=pltpu.VMEM),
        scratch_shapes=[
            vmem((TOK, CH), BF16),
            vmem((TOK, CH), BF16),
            vmem((TOK, CH), BF16),
            vmem((CHUNKS, TOK, LANES), F32),
            vmem((1, CH), F32),
            vmem((output_weight.shape[0], FEATURES), BF16),
            *[vmem(table.shape, table.dtype) for table in constants],
            vmem((CHUNKS, TOK, LANES), F32),
            vmem((CHUNKS, CTX, PER, 2 * LANES), BF16),
            vmem((CHUNKS, CTX, PER, 2 * LANES), BF16),
            vmem((2 * ROWS, 2 * LANES), BF16),
            vmem((CHUNKS, ROWS, LANES), BF16),
            vmem((CHUNKS, CTX, PER, LANES), BF16),
            vmem((TOK, LANES), F32),
            vmem((SIDE, 2, CHUNKS, TOK, LANES), BF16),
            vmem((TOK, FEATURES), F32),
            dma((13,)),
            dma((CHUNKS, CTX)),
            dma((CHUNKS, CTX)),
            dma((CHUNKS, CTX)),
            dma((CHUNKS, CTX)),
            dma((CHUNKS, 6)),
            dma((CHUNKS, 6)),
            dma((CHUNKS, SIDE, 2)),
            dma((CHUNKS, SIDE, 2)),
        ],
        compiler_params=pltpu.CompilerParams(
            collective_id=0, has_side_effects=True, vmem_limit_bytes=48 * 1024 * 1024
        ),
        cost_estimate=pl.CostEstimate(flops=3 * 10**9, bytes_accessed=8 * 10**6, transcendentals=0),
        name="hyena",
    )(*operands)


def solution(mesh):
    in_specs = (P("ctx", "ch"), P("ctx", "ch"), P("ctx", "ch"), P("ctx", "ch"), P("ch"), P())
    out_specs = P("ctx", "ch")
    return jax.shard_map(
        on_device, mesh=mesh, in_specs=in_specs, out_specs=out_specs, check_vma=False
    )
```

time: 699 us -> 50.4 us (0.07); the launches traced: 691 us -> 49.9 us
  waiting for transfers between devices: 565 us -> 0 us
  matrix products: 47.6 us -> 0 us
  other arithmetic: 44.9 us -> 0 us
  Pallas kernels: 0 us -> 39.1 us
  starting transfers between devices: 16.9 us -> 0 us
  between operations: 14.1 us -> 0.02 us
  local copies, waits for them, and re-layouts: 2.36 us -> 10.8 us
    ppermute x8 -> x0, waiting for transfers between devices: 526 us -> none  [partner_2(): return lax.ppermute(value, axis, pairs)]
    dot_general x9 -> x0, matrix products: 47.6 us -> none  [the longest x4 22.3 us: complex_apply(): direct = jnp.einsum(pattern, table_real, packed, precision=precise)]
    pallas_call x0 -> x1, Pallas kernels: none -> 39.1 us  [on_device(): pl.pallas_call(kernel, out_shape=jax.ShapeDtypeStruct((TOK, FEATURES), BF...]
    reduce_scatter x1 -> x0, waiting for transfers between devices: 38.9 us -> none  [on_device(): lax.psum_scatter(lax.dot_general(weight_rows, gated_rows, (((0,), (1,)),...]
    add x8 -> x0, other arithmetic: 19.6 us -> none  [the longest x4 16.3 us: butterfly_convolve(): current = rotate(partner + factor_sign * current, level_cosine, level_sine)]
    ppermute x8 -> x0, starting transfers between devices: 16.9 us -> none  [partner_2(): return lax.ppermute(value, axis, pairs)]
    concatenate x11 -> x0, other arithmetic: 12 us -> none  [the longest x10 11.7 us: rotate(): jnp.concatenate([real_part * cosine_part - imag_part * sine_part, real_pa...]
    unnamed x18 -> x21, local copies, waits for them, and re-layouts: 0.14 us -> 10.8 us
  transfers between devices with their start and end apart: 9 -> 0, of which waited for: 9 -> 0; matrix products, arithmetic and copies ran while one was open for 0% -> 0% of each run, Pallas kernels for 0% -> 0%
where the time goes in v1:
time: 50.4 us; the launch traced here: 49.9 us
  Pallas kernels  39.1 us (78%)
  local copies, waits for them, and re-layouts  10.8 us (21%)
    pallas_call x1, Pallas kernels, on_device(): pl.pallas_call(kernel, out_shape=jax.ShapeDtypeStruct((TOK, FEATURES), BF...  39.1 us
    unnamed x21, local copies, waits for them, and re-layouts  10.8 us

profile of v1, /device:TPU:1, one launch (start us, length us, event | category | flops | bytes accessed | tf_op | source)
XLA Modules:
  0.0 49.9 jit_solution(4164750062785569801)
XLA Ops:
  0.0 0.0 copy-start
  0.0 1.6 %copy-done = bf16[2,1024,512]{2,1,0:T(8,128)(2,1)S(1)} copy-done((bf16[2,1024,512]{2,1,0:T(8,128)(2,1)S(1)}, bf16[2,1024,512]{2,1,0:T(8,128)(2,1)}, u32[]{:S(2)}) %copy-start) | copy-done | bytes 2097176
  1.6 0.0 copy-start.1
  1.6 1.0 %copy-done.1 = f32[512,256]{1,0:T(8,128)S(1)} copy-done((f32[512,256]{1,0:T(8,128)S(1)}, f32[512,256]{1,0:T(8,128)}, u32[]{:S(2)}) %copy-start.1) | copy-done | bytes 524312
  2.6 0.0 copy-start.2
  2.6 1.0 %copy-done.2 = f32[2,512,128]{2,1,0:T(8,128)S(1)} copy-done((f32[2,512,128]{2,1,0:T(8,128)S(1)}, f32[2,512,128]{2,1,0:T(8,128)}, u32[]{:S(2)}) %copy-start.2) | copy-done | bytes 524312
  3.7 0.0 copy-start.3
  3.7 1.0 %copy-done.3 = f32[2,512,128]{2,1,0:T(8,128)S(1)} copy-done((f32[2,512,128]{2,1,0:T(8,128)S(1)}, f32[2,512,128]{2,1,0:T(8,128)}, u32[]{:S(2)}) %copy-start.3) | copy-done | bytes 524312
  4.7 0.0 copy-start.4
  4.7 0.9 %copy-done.4 = bf16[512,256]{1,0:T(8,128)(2,1)S(1)} copy-done((bf16[512,256]{1,0:T(8,128)(2,1)S(1)}, bf16[512,256]{1,0:T(8,128)(2,1)}, u32[]{:S(2)}) %copy-start.4) | copy-done | bytes 262168
  5.7 0.0 copy-start.5
  5.7 0.9 %copy-done.5 = bf16[512,256]{1,0:T(8,128)(2,1)S(1)} copy-done((bf16[512,256]{1,0:T(8,128)(2,1)S(1)}, bf16[512,256]{1,0:T(8,128)(2,1)}, u32[]{:S(2)}) %copy-start.5) | copy-done | bytes 262168
  6.6 0.0 copy-start.6
  6.6 0.9 %copy-done.6 = bf16[512,256]{1,0:T(8,128)(2,1)S(1)} copy-done((bf16[512,256]{1,0:T(8,128)(2,1)S(1)}, bf16[512,256]{1,0:T(8,128)(2,1)}, u32[]{:S(2)}) %copy-start.6) | copy-done | bytes 262168
  7.6 0.0 copy-start.7
  7.6 0.9 %copy-done.7 = bf16[2,256,256]{2,1,0:T(8,128)(2,1)S(1)} copy-done((bf16[2,256,256]{2,1,0:T(8,128)(2,1)S(1)}, bf16[2,256,256]{2,1,0:T(8,128)(2,1)}, u32[]{:S(2)}) %copy-start.7) | copy-done | bytes 262168
  8.5 0.0 copy-start.8
  8.5 0.9 %copy-done.8 = bf16[2,256,256]{2,1,0:T(8,128)(2,1)S(1)} copy-done((bf16[2,256,256]{2,1,0:T(8,128)(2,1)S(1)}, bf16[2,256,256]{2,1,0:T(8,128)(2,1)}, u32[]{:S(2)}) %copy-start.8) | copy-done | bytes 262168
  9.5 0.0 copy-start.9
  9.5 0.7 %copy-done.9 = f32[256]{0:T(256)S(1)} copy-done((f32[256]{0:T(256)S(1)}, f32[256]{0:T(256)}, u32[]{:S(2)}) %copy-start.9) | copy-done | bytes 1048
  10.2 39.1 %hyena.1 = bf16[512,256]{1,0:T(8,128)(2,1)S(1)} custom-call(bf16[512,256]{1,0:T(8,128)(2,1)S(1)} %copy-done.4, bf16[512,256]{1,0:T(8,128)(2,1)S(1)} %copy-done.5, bf16[512,256]{1,0:T(8,128)(2,1)S(1)} %copy-done.6, f32[512,256]{1,0:T(8,128)S(1)} %copy-done.1, f32[1,256]{1,0:T(1,128)S(1)} %bitcast.1, bf16[2048,2048]{1,0:T(8,128)(2,1)} %weight.1, ...), custom_call_target="tpu_custom_call" | custom-call | flops 3000000000 | bytes 8000000 | tf_op jit(solution)/shard_map/hyena/pallas_call | solution.py:348
  49.2 0.7 %copy.14 = bf16[512,256]{1,0:T(8,128)(2,1)} copy(bf16[512,256]{1,0:T(8,128)(2,1)S(1)} %hyena.1) | data formatting | bytes 524288
Async XLA Ops:
  0.0 1.6 %copy-start = (bf16[2,1024,512]{2,1,0:T(8,128)(2,1)S(1)}, bf16[2,1024,512]{2,1,0:T(8,128)(2,1)}, u32[]{:S(2)}) copy-start(bf16[2,1024,512]{2,1,0:T(8,128)(2,1)} %constant.12.clone.row_f) | copy-start | bytes 6291460
  1.6 1.0 %copy-start.1 = (f32[512,256]{1,0:T(8,128)S(1)}, f32[512,256]{1,0:T(8,128)}, u32[]{:S(2)}) copy-start(f32[512,256]{1,0:T(8,128)} %taps.1) | copy-start | bytes 1572868
  2.6 1.0 %copy-start.2 = (f32[2,512,128]{2,1,0:T(8,128)S(1)}, f32[2,512,128]{2,1,0:T(8,128)}, u32[]{:S(2)}) copy-start(f32[2,512,128]{2,1,0:T(8,128)} %constant.15.clone.untwid) | copy-start | bytes 1572868
  3.7 1.0 %copy-start.3 = (f32[2,512,128]{2,1,0:T(8,128)S(1)}, f32[2,512,128]{2,1,0:T(8,128)}, u32[]{:S(2)}) copy-start(f32[2,512,128]{2,1,0:T(8,128)} %constant.14.clone.twid) | copy-start | bytes 1572868
  4.7 0.9 %copy-start.4 = (bf16[512,256]{1,0:T(8,128)(2,1)S(1)}, bf16[512,256]{1,0:T(8,128)(2,1)}, u32[]{:S(2)}) copy-start(bf16[512,256]{1,0:T(8,128)(2,1)} %inner.1) | copy-start | bytes 786436
  5.7 0.9 %copy-start.5 = (bf16[512,256]{1,0:T(8,128)(2,1)S(1)}, bf16[512,256]{1,0:T(8,128)(2,1)}, u32[]{:S(2)}) copy-start(bf16[512,256]{1,0:T(8,128)(2,1)} %outer.1) | copy-start | bytes 786436
  6.6 0.9 %copy-start.6 = (bf16[512,256]{1,0:T(8,128)(2,1)S(1)}, bf16[512,256]{1,0:T(8,128)(2,1)}, u32[]{:S(2)}) copy-start(bf16[512,256]{1,0:T(8,128)(2,1)} %source.1) | copy-start | bytes 786436
  7.6 0.9 %copy-start.7 = (bf16[2,256,256]{2,1,0:T(8,128)(2,1)S(1)}, bf16[2,256,256]{2,1,0:T(8,128)(2,1)}, u32[]{:S(2)}) copy-start(bf16[2,256,256]{2,1,0:T(8,128)(2,1)} %constant.17.clone.ph_i) | copy-start | bytes 786436
  8.5 0.9 %copy-start.8 = (bf16[2,256,256]{2,1,0:T(8,128)(2,1)S(1)}, bf16[2,256,256]{2,1,0:T(8,128)(2,1)}, u32[]{:S(2)}) copy-start(bf16[2,256,256]{2,1,0:T(8,128)(2,1)} %constant.16.clone.ph_f) | copy-start | bytes 786436
  9.5 0.7 %copy-start.9 = (f32[256]{0:T(256)S(1)}, f32[256]{0:T(256)}, u32[]{:S(2)}) copy-start(f32[256]{0:T(256)} %param.16) | copy-start | bytes 3076

commit v2 on v1

--- a/solution.py
+++ b/solution.py
@@ -134,7 +134,7 @@
             ]
         )
     ]
-    for load in loads:
+    for load in loads[:4]:
         load.start()
 
     barrier = pltpu.get_barrier_semaphore()
@@ -172,6 +172,9 @@
         for k in far_first:
             a_copy(chunk, k).start()
         recv[chunk, me] = send[chunk, me]
+        if chunk == 0:
+            for load in loads[4:]:
+                load.start()
 
     def b_copy(chunk, k):
         to = peer(k)
@@ -348,7 +351,7 @@
     return pl.pallas_call(
         kernel,
         out_shape=jax.ShapeDtypeStruct((TOK, FEATURES), BF16),
-        in_specs=[pl.BlockSpec(memory_space=pl.ANY)] * len(operands),
+        in_specs=[pl.BlockSpec(memory_space=pltpu.HBM)] * len(operands),
         out_specs=pl.BlockSpec(memory_space=pltpu.VMEM),
         scratch_shapes=[
             vmem((TOK, CH), BF16),
@@ -382,7 +385,7 @@
         ),
         cost_estimate=pl.CostEstimate(flops=3 * 10**9, bytes_accessed=8 * 10**6, transcendentals=0),
         name="hyena",
-    )(*operands)
+    )(*[pltpu.with_memory_space_constraint(operand, pltpu.HBM) for operand in operands])
 
 
 def solution(mesh):

time: 50.4 us -> 39.5 us (0.78)
  local copies, waits for them, and re-layouts: 10.8 us -> 0.71 us
    unnamed x21 -> x1, local copies, waits for them, and re-layouts: 10.8 us -> 0.71 us
where the time goes in v2:
time: 39.5 us; the launch traced here: 39.4 us
  Pallas kernels  38.7 us (98%)
  local copies, waits for them, and re-layouts  0.71 us (2%)
    pallas_call x1, Pallas kernels, on_device(): pl.pallas_call(kernel, out_shape=jax.ShapeDtypeStruct((TOK, FEATURES), BF...  38.7 us

profile of v2, /device:TPU:1, one launch (start us, length us, event | category | flops | bytes accessed | tf_op | source)
XLA Modules:
  0.0 39.4 jit_solution(409834011489562035)
XLA Ops:
  0.0 38.7 %hyena.1 = bf16[512,256]{1,0:T(8,128)(2,1)S(1)} custom-call(bf16[512,256]{1,0:T(8,128)(2,1)} %inner.1, bf16[512,256]{1,0:T(8,128)(2,1)} %outer.1, bf16[512,256]{1,0:T(8,128)(2,1)} %source.1, f32[512,256]{1,0:T(8,128)} %taps.1, f32[1,256]{1,0:T(1,128)} %bitcast.1, bf16[2048,2048]{1,0:T(8,128)(2,1)} %weight.1, bf16[2,1024,512]{2,1,0:T(8,128)(2,1)} %constant.12.clone.row_f, ...), custom_call_target="tpu_custom_call" | custom-call | flops 3000000000 | bytes 8000000 | tf_op jit(solution)/shard_map/hyena/pallas_call | solution.py:351
  38.7 0.7 %copy.14 = bf16[512,256]{1,0:T(8,128)(2,1)} copy(bf16[512,256]{1,0:T(8,128)(2,1)S(1)} %hyena.1) | data formatting | bytes 524288

commit v3 on v2

v3 whole, which is shorter than its diff:
```python
import functools

import jax
import jax.numpy as jnp
import ml_dtypes
import numpy as np
from jax import lax
from jax.experimental import pallas as pl
from jax.experimental.pallas import tpu as pltpu
from jax.sharding import PartitionSpec as P

MESH = pl.DeviceIdType.MESH
F32 = jnp.float32
BF16 = jnp.bfloat16

CTX = 16
SIDE = 4
TOK = 512
CH = 256
LANES = 128
TILES = 2
SUBS = 4
GROUP = 4
PHASES = 32
PER = TOK // PHASES
ROWS = CTX * PER
LENGTH = ROWS * PHASES
FEATURES = 256
HALF = TOK // 2
PIECE = HALF // 2
BLOCK = 128


def split_table(table, axis):
    high = table.astype(np.float32).astype(ml_dtypes.bfloat16)
    low = (table - high.astype(np.float64)).astype(np.float32).astype(ml_dtypes.bfloat16)
    if axis == 1:
        return np.concatenate([high, low], axis=1)
    return np.concatenate([high, high, low], axis=0)


def tables():
    k_row = np.arange(ROWS) + 0.25
    rows = np.arange(ROWS)
    turn = 2.0 * np.pi * np.outer(k_row, rows) / ROWS
    row_forward = np.concatenate([np.cos(turn), -np.sin(turn)], axis=0)
    row_inverse = np.concatenate([np.cos(turn.T), -np.sin(turn.T)], axis=1)
    phase = np.repeat(np.arange(PHASES), GROUP)
    twist = 2.0 * np.pi * np.outer(k_row, phase) / LENGTH
    twiddle = np.stack([np.cos(twist), -np.sin(twist)]).astype(np.float32)
    untwiddle = (np.stack([np.cos(twist), np.sin(twist)]) / LENGTH).astype(np.float32)
    angle = 2.0 * np.pi * np.outer(np.arange(PHASES), np.arange(PHASES)) / PHASES
    cosine = np.kron(np.cos(angle), np.eye(GROUP))
    sine = np.kron(np.sin(angle), np.eye(GROUP))
    phase_forward = np.block([[cosine, -sine], [sine, cosine]])
    phase_inverse = np.block([[cosine, sine], [-sine, cosine]])
    return (
        split_table(row_forward, 1),
        split_table(row_inverse, 1),
        twiddle,
        untwiddle,
        split_table(phase_forward, 0),
        split_table(phase_inverse, 0),
    )


def lane_bit(shape, width):
    return (lax.broadcasted_iota(jnp.int32, shape, 1) & width) != 0


def swap_groups(parts, roll):
    parts = list(parts)
    bit = CTX // 2
    while bit:
        shift = bit * GROUP
        upper = lane_bit(parts[0].shape, shift)
        for j in range(CTX):
            if j & bit:
                continue
            first, second = parts[j], parts[j | bit]
            parts[j] = jnp.where(upper, roll(second, shift), first)
            parts[j | bit] = jnp.where(upper, second, roll(first, LANES - shift))
        bit //= 2
    return parts


def pack(rows_of, e, roll):
    parts = []
    for j in range(CTX):
        first, second = rows_of(j), rows_of(j + CTX)
        upper = lane_bit(first.shape, LANES // 2)
        if e == 0:
            parts.append(jnp.where(upper, roll(second, LANES // 2), first))
        else:
            parts.append(jnp.where(upper, second, roll(first, LANES // 2)))
    return swap_groups(parts, roll)


def halves(rows, e):
    blocks = rows.reshape(PER, 2, PHASES // 2, LANES)
    first, second = blocks[:, 0].reshape(HALF, LANES), blocks[:, 1].reshape(HALF, LANES)
    upper = lane_bit(first.shape, LANES // 2)
    if e == 0:
        return jnp.where(upper, pltpu.roll(second, LANES // 2, 1), first)
    return jnp.where(upper, second, pltpu.roll(first, LANES // 2, 1))


def lane_roll(value, shift):
    return pltpu.roll(value, shift, 1)


def split(value):
    high = value.astype(BF16)
    return high, (value - high.astype(F32)).astype(BF16)


def dot(a, b):
    return jnp.dot(a, b, preferred_element_type=F32)


def dot3(value, table):
    high, low = split(value)
    return dot(jnp.concatenate([high, low, high], axis=1), table[...])


def kernel(
    inner, outer, source, taps, skip, weight, row_f, row_i, twid, untwid, ph_f, ph_i,
    out,
    v_inner, v_outer, v_source, v_taps, v_skip, v_weight, v_row_f, v_row_i, v_twid, v_untwid, v_ph_f, v_ph_i,
    signal, send, recv, y_send, y_recv, y_full, gates, skipped, gated, acc,
    load_sem, a_send, a_recv, b_send, b_recv, c_send, c_recv, s_send, s_recv,
):
    me = lax.axis_index("ctx")
    rank = lax.axis_index("ch")
    x_me, z_me = me // SIDE, me % SIDE
    y_me, core = rank // 2, rank % 2
    up = lax.rem(y_me + 1, SIDE) * 2 + core
    down = lax.rem(y_me + SIDE - 1, SIDE) * 2 + core
    sibling = y_me * 2 + (1 - core)

    def peer(k):
        return lax.rem(x_me + k // SIDE, SIDE) * SIDE + lax.rem(z_me + k % SIDE, SIDE)

    feature0 = pl.multiple_of(rank * FEATURES, FEATURES)
    pairs = []
    for tile in range(TILES):
        lanes = pl.ds(tile * LANES, LANES)
        pairs += [(src.at[:, lanes], dst.at[tile]) for src, dst in ((taps, v_taps), (inner, v_inner), (source, v_source))]
    pairs += [(row_f, v_row_f), (twid, v_twid), (ph_f, v_ph_f), (ph_i, v_ph_i), (untwid, v_untwid), (row_i, v_row_i)]
    pairs += [(outer, v_outer), (skip, v_skip), (weight.at[:, pl.ds(feature0, FEATURES)], v_weight)]
    loads = [pltpu.make_async_copy(src, dst, load_sem.at[n]) for n, (src, dst) in enumerate(pairs)]
    for load in loads[:6]:
        load.start()

    barrier = pltpu.get_barrier_semaphore()
    for k in range(1, CTX):
        pl.semaphore_signal(barrier, inc=1, device_id=(peer(k), rank), device_id_type=MESH)
    for other in (up, down, sibling):
        pl.semaphore_signal(barrier, inc=1, device_id=(me, other), device_id_type=MESH)

    far_first = sorted(range(1, CTX), key=lambda k: -(2 - abs(2 - k // SIDE)) - (2 - abs(2 - k % SIDE)))

    def a_copy(chunk, k):
        to = peer(k)
        return pltpu.make_async_remote_copy(
            src_ref=send.at[chunk, to],
            dst_ref=recv.at[chunk, me],
            send_sem=a_send.at[chunk, k],
            recv_sem=a_recv.at[chunk, k],
            device_id=(to, rank),
            device_id_type=MESH,
        )

    for chunk in range(SUBS):
        tile, e = chunk // 2, chunk % 2
        if e == 0:
            for load in loads[3 * tile : 3 * tile + 3]:
                load.wait()
            signal[tile] = v_inner[tile].astype(F32) * v_source[tile].astype(F32)
        for place, ref in enumerate((signal, v_taps)):
            parts = pack(lambda q: ref[tile, pl.ds(q, PER, stride=PHASES), :], e, lane_roll)
            for d in range(CTX):
                send[chunk, d, :, place * LANES : (place + 1) * LANES] = parts[d].astype(BF16)
        if chunk == 0:
            pl.semaphore_wait(barrier, CTX + 2)
        for k in far_first:
            a_copy(chunk, k).start()
        recv[chunk, me] = send[chunk, me]
        if chunk == 1:
            for load in loads[6:]:
                load.start()

    def b_copy(chunk, k):
        to = peer(k)
        return pltpu.make_async_remote_copy(
            src_ref=y_send.at[chunk, to],
            dst_ref=y_recv.at[chunk, me],
            send_sem=b_send.at[chunk, k],
            recv_sem=b_recv.at[chunk, k],
            device_id=(to, rank),
            device_id_type=MESH,
        )

    def convolve(chunk):
        for k in range(1, CTX):
            a_copy(chunk, k).wait_recv()
        if chunk == 0:
            for load in loads[6:12]:
                load.wait()
        arrived = recv[chunk].reshape(ROWS, 2 * LANES)
        arrived = jnp.concatenate([arrived, arrived], axis=0)
        starts = range(0, ROWS, BLOCK)
        staged = [
            (dot(v_row_f[start : start + BLOCK], arrived), dot(v_row_f[ROWS + start : ROWS + start + BLOCK], arrived))
            for start in starts
        ]
        spectra = []
        for start, (real, imag) in zip(starts, staged):
            cosine, sine = v_twid[0, start : start + BLOCK], v_twid[1, start : start + BLOCK]
            turned = []
            for place in (0, 1):
                re = real[:, place * LANES : (place + 1) * LANES]
                im = imag[:, place * LANES : (place + 1) * LANES]
                turned.append(jnp.concatenate([re * cosine - im * sine, re * sine + im * cosine], axis=1))
            spectra.append(dot3(jnp.concatenate(turned, axis=0), v_ph_f))
        backs = []
        for both in spectra:
            xr, xi = both[:BLOCK, :LANES], both[:BLOCK, LANES:]
            hr, hi = both[BLOCK:, :LANES], both[BLOCK:, LANES:]
            backs.append(dot3(jnp.concatenate([xr * hr - xi * hi, xr * hi + xi * hr], axis=1), v_ph_i))
        reals, imags = [], []
        for start, back in zip(starts, backs):
            re, im = back[:, :LANES], back[:, LANES:]
            cosine, sine = v_untwid[0, start : start + BLOCK], v_untwid[1, start : start + BLOCK]
            reals.append(jnp.concatenate(split(re * cosine - im * sine), axis=1))
            imags.append(jnp.concatenate(split(re * sine + im * cosine), axis=1))
        spectrum = jnp.concatenate(reals + imags, axis=0)
        spectrum = jnp.concatenate([spectrum, spectrum], axis=0)
        side_rows = SIDE * PER
        for pair in ((2, 1), (3, 0)):
            to_x = [lax.rem(x_me + dx, SIDE) for dx in pair]
            left = [v_row_i[pl.ds(pl.multiple_of(x * side_rows, side_rows), side_rows), :] for x in to_x]
            wide = dot(jnp.concatenate(left, axis=0), spectrum)
            y = (wide[:, :LANES] + wide[:, LANES:]).astype(BF16)
            for n, dx in enumerate(pair):
                block = y[n * side_rows : (n + 1) * side_rows].reshape(SIDE, PER, LANES)
                y_send[chunk, pl.ds(to_x[n] * SIDE, SIDE)] = block
                for dz in (2, 1, 3, 0):
                    if dx or dz:
                        b_copy(chunk, dx * SIDE + dz).start()
        y_recv[chunk, me] = y_send[chunk, me]

    def piece(ref, p):
        return ref.at[pl.ds(p * PIECE, PIECE)]

    def ring(chunk, name, p):
        frm, slot, column, device, index = {
            "up": (0, 1, 0, up, 0),
            "down": (0, 3, 0, down, 1),
            "far": ((1, 3)[p], 2, 0, (up, down)[p], 2),
            "cross": ((1, 3)[p], 2, 1, (up, down)[p], 3),
        }[name]
        return pltpu.make_async_remote_copy(
            src_ref=piece(gated.at[frm, column, chunk], p),
            dst_ref=piece(gated.at[slot, column, chunk], p),
            send_sem=c_send.at[chunk, index, p],
            recv_sem=c_recv.at[chunk, index, p],
            device_id=(me, device),
            device_id_type=MESH,
        )

    def pair(chunk, slot, p, column=0):
        return pltpu.make_async_remote_copy(
            src_ref=piece(gated.at[slot, column, chunk], p),
            dst_ref=piece(gated.at[slot, 1 - column, chunk], p),
            send_sem=s_send.at[chunk, slot + 2 * column, p],
            recv_sem=s_recv.at[chunk, slot + 2 * column, p],
            device_id=(me, sibling),
            device_id_type=MESH,
        )

    first_core, second_core = core == 0, core == 1

    def prepare():
        for load in loads[12:14]:
            load.wait()
        for chunk in range(SUBS):
            tile, e = chunk // 2, chunk % 2
            lanes = slice(tile * LANES, (tile + 1) * LANES)
            gates[chunk] = halves(v_outer[:, lanes].astype(F32), e)
            skipped[chunk] = halves(v_skip[0:1, lanes] * signal[tile], e)

    def gate(chunk):
        for k in range(1, CTX):
            b_copy(chunk, k).wait_recv()
        parts = swap_groups([y_recv[chunk, d].astype(F32) for d in range(CTX)], lane_roll)
        for j in range(CTX):
            y_full[pl.ds(j, PER, stride=CTX), :] = parts[j]
        gated[0, 0, chunk] = (gates[chunk] * (y_full[...] + skipped[chunk])).astype(BF16)
        for p in (0, 1):
            ring(chunk, "up", p).start()
            ring(chunk, "down", 1 - p).start()
        for p in (0, 1):
            pair(chunk, 0, p).start()

    def near(chunk):
        for name, slot, p in (("up", 1, 0), ("down", 3, 1)):
            ring(chunk, name, p).wait_recv()
            pair(chunk, slot, p).start()

            @pl.when(second_core)
            def _(p=p):
                ring(chunk, "far", p).start()

        for name, slot, p in (("up", 1, 1), ("down", 3, 0)):
            ring(chunk, name, p).wait_recv()
            pair(chunk, slot, p).start()

    def cross(chunk):
        @pl.when(second_core)
        def _():
            for slot, p in ((1, 0), (3, 1)):
                pair(chunk, slot, p).wait_recv()
                ring(chunk, "cross", p).start()

    def far(chunk):
        @pl.when(second_core)
        def _():
            for column, name in enumerate(("far", "cross")):
                for p in (0, 1):
                    ring(chunk, name, p).wait_recv()
                    pair(chunk, 2, p, column).start()

    def arrived_pairs(chunk, slot):
        if slot == 0:
            for p in (0, 1):
                pair(chunk, 0, p).wait_recv()
        elif slot == 2:

            @pl.when(first_core)
            def _():
                for column in (0, 1):
                    for p in (0, 1):
                        pair(chunk, 2, p, column).wait_recv()

        else:
            ahead = 0 if slot == 1 else 1

            @pl.when(first_core)
            def _():
                pair(chunk, slot, ahead).wait_recv()

            pair(chunk, slot, 1 - ahead).wait_recv()

    def project(chunk, slot, first=False, last=False):
        arrived_pairs(chunk, slot)
        if chunk == 0 and slot == 0:
            loads[14].wait()
        y_from = lax.rem(y_me + SIDE - slot, SIDE)
        width = LANES // 2
        right = []
        for c in (core, 1 - core):
            start = pl.multiple_of((2 * y_from + c) * CH + chunk * width, width)
            right += [v_weight[pl.ds(start, width), :]] * 2
        left = jnp.concatenate([gated[slot, 0, chunk], gated[slot, 1, chunk]], axis=1)
        upper = lane_bit(left.shape, width)
        none = jnp.zeros_like(left)
        left = jnp.concatenate([jnp.where(upper, none, left), jnp.where(upper, left, none)], axis=0)
        term = dot(left, jnp.concatenate(right, axis=0))
        if not first:
            term = acc[...] + term
        if last:
            rows = term.astype(BF16).reshape(2, PER, PHASES // 2, FEATURES)
            for h in (0, 1):
                for r in range(PER):
                    start = r * PHASES + h * (PHASES // 2)
                    out[start : start + PHASES // 2] = rows[h, r]
        else:
            acc[...] = term

    prepare()
    for chunk in range(SUBS):
        convolve(chunk)
    for chunk in range(SUBS):
        gate(chunk)
    near(0)
    near(1)
    near(2)
    cross(0)
    project(0, 0, first=True)
    near(3)
    cross(1)
    project(1, 0)
    cross(2)
    far(0)
    project(2, 0)
    project(0, 1)
    project(0, 3)
    cross(3)
    far(1)
    project(3, 0)
    project(1, 1)
    project(1, 3)
    far(2)
    project(0, 2)
    project(2, 1)
    project(2, 3)
    far(3)
    project(1, 2)
    project(3, 1)
    project(3, 3)
    project(2, 2)
    project(3, 2, last=True)

    for chunk in range(SUBS):
        for k in range(1, CTX):
            a_copy(chunk, k).wait_send()
            b_copy(chunk, k).wait_send()
        for p in (0, 1):
            ring(chunk, "up", p).wait_send()
            ring(chunk, "down", p).wait_send()
            for slot in (0, 1, 3):
                pair(chunk, slot, p).wait_send()

    @pl.when(second_core)
    def _():
        for chunk in range(SUBS):
            for p in (0, 1):
                ring(chunk, "far", p).wait_send()
                ring(chunk, "cross", p).wait_send()
                for column in (0, 1):
                    pair(chunk, 2, p, column).wait_send()


def on_device(inner_gate, outer_gate, source_values, filter_taps, skip_gain, output_weight):
    constants = [jnp.asarray(table) for table in tables()]
    operands = (inner_gate, outer_gate, source_values, filter_taps, skip_gain.reshape(1, CH), output_weight, *constants)
    vmem = pltpu.VMEM
    dma = pltpu.SemaphoreType.DMA
    return pl.pallas_call(
        kernel,
        out_shape=jax.ShapeDtypeStruct((TOK, FEATURES), BF16),
        in_specs=[pl.BlockSpec(memory_space=pltpu.HBM)] * len(operands),
        out_specs=pl.BlockSpec(memory_space=pltpu.VMEM),
        scratch_shapes=[
            vmem((TILES, TOK, LANES), BF16),
            vmem((TOK, CH), BF16),
            vmem((TILES, TOK, LANES), BF16),
            vmem((TILES, TOK, LANES), F32),
            vmem((1, CH), F32),
            vmem((output_weight.shape[0], FEATURES), BF16),
            *[vmem(table.shape, table.dtype) for table in constants],
            vmem((TILES, TOK, LANES), F32),
            vmem((SUBS, CTX, PER, 2 * LANES), BF16),
            vmem((SUBS, CTX, PER, 2 * LANES), BF16),
            vmem((SUBS, CTX, PER, LANES), BF16),
            vmem((SUBS, CTX, PER, LANES), BF16),
            vmem((HALF, LANES), F32),
            vmem((SUBS, HALF, LANES), F32),
            vmem((SUBS, HALF, LANES), F32),
            vmem((SIDE, 2, SUBS, HALF, LANES), BF16),
            vmem((TOK, FEATURES), F32),
            dma((15,)),
            dma((SUBS, CTX)),
            dma((SUBS, CTX)),
            dma((SUBS, CTX)),
            dma((SUBS, CTX)),
            dma((SUBS, 4, 2)),
            dma((SUBS, 4, 2)),
            dma((SUBS, 5, 2)),
            dma((SUBS, 5, 2)),
        ],
        compiler_params=pltpu.CompilerParams(
            collective_id=0, has_side_effects=True, vmem_limit_bytes=48 * 1024 * 1024
        ),
        cost_estimate=pl.CostEstimate(flops=3 * 10**9, bytes_accessed=8 * 10**6, transcendentals=0),
        name="hyena",
    )(*[pltpu.with_memory_space_constraint(operand, pltpu.HBM) for operand in operands])


def solution(mesh):
    in_specs = (P("ctx", "ch"), P("ctx", "ch"), P("ctx", "ch"), P("ctx", "ch"), P("ch"), P())
    out_specs = P("ctx", "ch")
    return jax.shard_map(
        on_device, mesh=mesh, in_specs=in_specs, out_specs=out_specs, check_vma=False
    )
```

time: 39.5 us -> 36.9 us (0.934)
  Pallas kernels: 38.7 us -> 36.1 us
    pallas_call x1, Pallas kernels: 38.7 us -> 36.1 us  [on_device(): pl.pallas_call(kernel, out_shape=jax.ShapeDtypeStruct((TOK, FEATURES), BF...]
where the time goes in v3:
time: 36.9 us; the launch traced here: 36.8 us
  Pallas kernels  36.1 us (98%)
  local copies, waits for them, and re-layouts  0.71 us (2%)
    pallas_call x1, Pallas kernels, on_device(): pl.pallas_call(kernel, out_shape=jax.ShapeDtypeStruct((TOK, FEATURES), BF...  36.1 us

profile of v3, /device:TPU:1, one launch (start us, length us, event | category | flops | bytes accessed | tf_op | source)
XLA Modules:
  0.0 36.8 jit_solution(4311499057280056475)
XLA Ops:
  0.0 36.1 %hyena.1 = bf16[512,256]{1,0:T(8,128)(2,1)S(1)} custom-call(bf16[512,256]{1,0:T(8,128)(2,1)} %inner.1, bf16[512,256]{1,0:T(8,128)(2,1)} %outer.1, bf16[512,256]{1,0:T(8,128)(2,1)} %source.1, f32[512,256]{1,0:T(8,128)} %taps.1, f32[1,256]{1,0:T(1,128)} %bitcast.1, bf16[2048,2048]{1,0:T(8,128)(2,1)} %weight.1, bf16[512,512]{1,0:T(8,128)(2,1)} %constant.12.clone.row_f, ...), custom_call_target="tpu_custom_call" | custom-call | flops 3000000000 | bytes 8000000 | tf_op jit(solution)/shard_map/hyena/pallas_call | solution.py:440
  36.1 0.7 %copy.14 = bf16[512,256]{1,0:T(8,128)(2,1)} copy(bf16[512,256]{1,0:T(8,128)(2,1)S(1)} %hyena.1) | data formatting | bytes 524288

commit v4 on v3

--- a/solution.py
+++ b/solution.py
@@ -160,13 +160,24 @@
 
     far_first = sorted(range(1, CTX), key=lambda k: -(2 - abs(2 - k // SIDE)) - (2 - abs(2 - k % SIDE)))
 
+    def all_of(ref, chunk, send_sem, recv_sem):
+        ref = ref.at[chunk, pl.ds(0, CTX - 1)]
+        return pltpu.make_async_remote_copy(
+            src_ref=ref,
+            dst_ref=ref,
+            send_sem=send_sem.at[chunk],
+            recv_sem=recv_sem.at[chunk],
+            device_id=(me, sibling),
+            device_id_type=MESH,
+        )
+
     def a_copy(chunk, k):
         to = peer(k)
         return pltpu.make_async_remote_copy(
             src_ref=send.at[chunk, to],
             dst_ref=recv.at[chunk, me],
-            send_sem=a_send.at[chunk, k],
-            recv_sem=a_recv.at[chunk, k],
+            send_sem=a_send.at[chunk],
+            recv_sem=a_recv.at[chunk],
             device_id=(to, rank),
             device_id_type=MESH,
         )
@@ -195,15 +206,14 @@
         return pltpu.make_async_remote_copy(
             src_ref=y_send.at[chunk, to],
             dst_ref=y_recv.at[chunk, me],
-            send_sem=b_send.at[chunk, k],
-            recv_sem=b_recv.at[chunk, k],
+            send_sem=b_send.at[chunk],
+            recv_sem=b_recv.at[chunk],
             device_id=(to, rank),
             device_id_type=MESH,
         )
 
     def convolve(chunk):
-        for k in range(1, CTX):
-            a_copy(chunk, k).wait_recv()
+        all_of(recv, chunk, a_send, a_recv).wait_recv()
         if chunk == 0:
             for load in loads[6:12]:
                 load.wait()
@@ -291,8 +301,7 @@
             skipped[chunk] = halves(v_skip[0:1, lanes] * signal[tile], e)
 
     def gate(chunk):
-        for k in range(1, CTX):
-            b_copy(chunk, k).wait_recv()
+        all_of(y_recv, chunk, b_send, b_recv).wait_recv()
         parts = swap_groups([y_recv[chunk, d].astype(F32) for d in range(CTX)], lane_roll)
         for j in range(CTX):
             y_full[pl.ds(j, PER, stride=CTX), :] = parts[j]
@@ -383,7 +392,11 @@
         convolve(chunk)
     for chunk in range(SUBS):
         gate(chunk)
+    for chunk in range(SUBS):
+        all_of(recv, chunk, a_send, a_recv).wait_send()
     near(0)
+    for chunk in range(SUBS):
+        all_of(y_recv, chunk, b_send, b_recv).wait_send()
     near(1)
     near(2)
     cross(0)
@@ -413,9 +426,6 @@
     project(3, 2, last=True)
 
     for chunk in range(SUBS):
-        for k in range(1, CTX):
-            a_copy(chunk, k).wait_send()
-            b_copy(chunk, k).wait_send()
         for p in (0, 1):
             ring(chunk, "up", p).wait_send()
             ring(chunk, "down", p).wait_send()
@@ -461,10 +471,10 @@
             vmem((SIDE, 2, SUBS, HALF, LANES), BF16),
             vmem((TOK, FEATURES), F32),
             dma((15,)),
-            dma((SUBS, CTX)),
-            dma((SUBS, CTX)),
-            dma((SUBS, CTX)),
-            dma((SUBS, CTX)),
+            dma((SUBS,)),
+            dma((SUBS,)),
+            dma((SUBS,)),
+            dma((SUBS,)),
             dma((SUBS, 4, 2)),
             dma((SUBS, 4, 2)),
             dma((SUBS, 5, 2)),

time: 36.9 us -> 34.7 us (0.940)
  Pallas kernels: 36.1 us -> 33.8 us
    pallas_call x1, Pallas kernels: 36.1 us -> 33.8 us  [on_device(): pl.pallas_call(kernel, out_shape=jax.ShapeDtypeStruct((TOK, FEATURES), BF...]
where the time goes in v4:
time: 34.7 us; the launch traced here: 34.5 us
  Pallas kernels  33.8 us (97%)
  local copies, waits for them, and re-layouts  0.71 us (2%)
    pallas_call x1, Pallas kernels, on_device(): pl.pallas_call(kernel, out_shape=jax.ShapeDtypeStruct((TOK, FEATURES), BF...  33.8 us
    unnamed x1, local copies, waits for them, and re-layouts  0.71 us

profile of v4, /device:TPU:1, one launch (start us, length us, event | category | flops | bytes accessed | tf_op | source)
XLA Modules:
  0.0 34.5 jit_solution(4324633050427896196)
XLA Ops:
  0.0 33.8 %hyena.1 = bf16[512,256]{1,0:T(8,128)(2,1)S(1)} custom-call(bf16[512,256]{1,0:T(8,128)(2,1)} %inner.1, bf16[512,256]{1,0:T(8,128)(2,1)} %outer.1, bf16[512,256]{1,0:T(8,128)(2,1)} %source.1, f32[512,256]{1,0:T(8,128)} %taps.1, f32[1,256]{1,0:T(1,128)} %bitcast.1, bf16[2048,2048]{1,0:T(8,128)(2,1)} %weight.1, bf16[512,512]{1,0:T(8,128)(2,1)} %constant.12.clone.row_f, ...), custom_call_target="tpu_custom_call" | custom-call | flops 3000000000 | bytes 8000000 | tf_op jit(solution)/shard_map/hyena/pallas_call | solution.py:450
  33.8 0.7 %copy.14 = bf16[512,256]{1,0:T(8,128)(2,1)} copy(bf16[512,256]{1,0:T(8,128)(2,1)S(1)} %hyena.1) | data formatting | bytes 524288

commit v5 on v4

--- a/solution.py
+++ b/solution.py
@@ -273,7 +273,7 @@
         return pltpu.make_async_remote_copy(
             src_ref=piece(gated.at[frm, column, chunk], p),
             dst_ref=piece(gated.at[slot, column, chunk], p),
-            send_sem=c_send.at[chunk, index, p],
+            send_sem=c_send.at[index // 2],
             recv_sem=c_recv.at[chunk, index, p],
             device_id=(me, device),
             device_id_type=MESH,
@@ -283,8 +283,18 @@
         return pltpu.make_async_remote_copy(
             src_ref=piece(gated.at[slot, column, chunk], p),
             dst_ref=piece(gated.at[slot, 1 - column, chunk], p),
-            send_sem=s_send.at[chunk, slot + 2 * column, p],
-            recv_sem=s_recv.at[chunk, slot + 2 * column, p],
+            send_sem=s_send.at[{0: 0, 1: 1, 3: 1, 2: 2}[slot]],
+            recv_sem=s_recv.at[chunk, 0, slot] if slot in (0, 2) else s_recv.at[chunk, 1 + p, slot],
+            device_id=(me, sibling),
+            device_id_type=MESH,
+        )
+
+    def together(ref, send_sem, recv_sem):
+        return pltpu.make_async_remote_copy(
+            src_ref=ref,
+            dst_ref=ref,
+            send_sem=send_sem,
+            recv_sem=recv_sem,
             device_id=(me, sibling),
             device_id_type=MESH,
         )
@@ -342,15 +352,12 @@
 
     def arrived_pairs(chunk, slot):
         if slot == 0:
-            for p in (0, 1):
-                pair(chunk, 0, p).wait_recv()
+            together(gated.at[0, 1, chunk], s_send.at[0], s_recv.at[chunk, 0, 0]).wait_recv()
         elif slot == 2:
 
             @pl.when(first_core)
             def _():
-                for column in (0, 1):
-                    for p in (0, 1):
-                        pair(chunk, 2, p, column).wait_recv()
+                together(gated.at[2, :, chunk], s_send.at[0], s_recv.at[chunk, 0, 2]).wait_recv()
 
         else:
             ahead = 0 if slot == 1 else 1
@@ -425,21 +432,17 @@
     project(2, 2)
     project(3, 2, last=True)
 
-    for chunk in range(SUBS):
-        for p in (0, 1):
-            ring(chunk, "up", p).wait_send()
-            ring(chunk, "down", p).wait_send()
-            for slot in (0, 1, 3):
-                pair(chunk, slot, p).wait_send()
+    def sent(ref, send_sem):
+        together(ref, send_sem, s_recv.at[0, 0, 0]).wait_send()
+
+    sent(gated.at[0], c_send.at[0])
+    sent(gated.at[0, 0], s_send.at[0])
+    sent(gated.at[0], s_send.at[1])
 
     @pl.when(second_core)
     def _():
-        for chunk in range(SUBS):
-            for p in (0, 1):
-                ring(chunk, "far", p).wait_send()
-                ring(chunk, "cross", p).wait_send()
-                for column in (0, 1):
-                    pair(chunk, 2, p, column).wait_send()
+        sent(gated.at[0], c_send.at[1])
+        sent(gated.at[0], s_send.at[2])
 
 
 def on_device(inner_gate, outer_gate, source_values, filter_taps, skip_gain, output_weight):
@@ -475,10 +478,10 @@
             dma((SUBS,)),
             dma((SUBS,)),
             dma((SUBS,)),
+            dma((2,)),
             dma((SUBS, 4, 2)),
-            dma((SUBS, 4, 2)),
-            dma((SUBS, 5, 2)),
-            dma((SUBS, 5, 2)),
+            dma((3,)),
+            dma((SUBS, 3, SIDE)),
         ],
         compiler_params=pltpu.CompilerParams(
             collective_id=0, has_side_effects=True, vmem_limit_bytes=48 * 1024 * 1024

time: 34.7 us -> 34 us (0.980)
  Pallas kernels: 33.8 us -> 33.2 us
    pallas_call x1, Pallas kernels: 33.8 us -> 33.2 us  [on_device(): pl.pallas_call(kernel, out_shape=jax.ShapeDtypeStruct((TOK, FEATURES), BF...]
where the time goes in v5:
time: 34 us; the launch traced here: 33.9 us
  Pallas kernels  33.2 us (98%)
  local copies, waits for them, and re-layouts  0.71 us (2%)
    pallas_call x1, Pallas kernels, on_device(): pl.pallas_call(kernel, out_shape=jax.ShapeDtypeStruct((TOK, FEATURES), BF...  33.2 us
    unnamed x1, local copies, waits for them, and re-layouts  0.71 us

profile of v5, /device:TPU:1, one launch (start us, length us, event | category | flops | bytes accessed | tf_op | source)
XLA Modules:
  0.0 33.9 jit_solution(16970367273417913331)
XLA Ops:
  0.0 33.2 %hyena.1 = bf16[512,256]{1,0:T(8,128)(2,1)S(1)} custom-call(bf16[512,256]{1,0:T(8,128)(2,1)} %inner.1, bf16[512,256]{1,0:T(8,128)(2,1)} %outer.1, bf16[512,256]{1,0:T(8,128)(2,1)} %source.1, f32[512,256]{1,0:T(8,128)} %taps.1, f32[1,256]{1,0:T(1,128)} %bitcast.1, bf16[2048,2048]{1,0:T(8,128)(2,1)} %weight.1, bf16[512,512]{1,0:T(8,128)(2,1)} %constant.12.clone.row_f, ...), custom_call_target="tpu_custom_call" | custom-call | flops 3000000000 | bytes 8000000 | tf_op jit(solution)/shard_map/hyena/pallas_call | solution.py:453
  33.2 0.7 %copy.14 = bf16[512,256]{1,0:T(8,128)(2,1)} copy(bf16[512,256]{1,0:T(8,128)(2,1)S(1)} %hyena.1) | data formatting | bytes 524288

commit v6 on v5

--- a/solution.py
+++ b/solution.py
@@ -165,7 +165,7 @@
         return pltpu.make_async_remote_copy(
             src_ref=ref,
             dst_ref=ref,
-            send_sem=send_sem.at[chunk],
+            send_sem=send_sem.at[0],
             recv_sem=recv_sem.at[chunk],
             device_id=(me, sibling),
             device_id_type=MESH,
@@ -176,7 +176,7 @@
         return pltpu.make_async_remote_copy(
             src_ref=send.at[chunk, to],
             dst_ref=recv.at[chunk, me],
-            send_sem=a_send.at[chunk],
+            send_sem=a_send.at[0],
             recv_sem=a_recv.at[chunk],
             device_id=(to, rank),
             device_id_type=MESH,
@@ -206,7 +206,7 @@
         return pltpu.make_async_remote_copy(
             src_ref=y_send.at[chunk, to],
             dst_ref=y_recv.at[chunk, me],
-            send_sem=b_send.at[chunk],
+            send_sem=b_send.at[0],
             recv_sem=b_recv.at[chunk],
             device_id=(to, rank),
             device_id_type=MESH,
@@ -274,7 +274,7 @@
             src_ref=piece(gated.at[frm, column, chunk], p),
             dst_ref=piece(gated.at[slot, column, chunk], p),
             send_sem=c_send.at[index // 2],
-            recv_sem=c_recv.at[chunk, index, p],
+            recv_sem=c_recv.at[chunk, 4 if index >= 2 else 2 * index + p],
             device_id=(me, device),
             device_id_type=MESH,
         )
@@ -284,7 +284,7 @@
             src_ref=piece(gated.at[slot, column, chunk], p),
             dst_ref=piece(gated.at[slot, 1 - column, chunk], p),
             send_sem=s_send.at[{0: 0, 1: 1, 3: 1, 2: 2}[slot]],
-            recv_sem=s_recv.at[chunk, 0, slot] if slot in (0, 2) else s_recv.at[chunk, 1 + p, slot],
+            recv_sem=s_recv.at[chunk, slot // 2 if slot in (0, 2) else slot + 1 + p],
             device_id=(me, sibling),
             device_id_type=MESH,
         )
@@ -345,19 +345,19 @@
     def far(chunk):
         @pl.when(second_core)
         def _():
-            for column, name in enumerate(("far", "cross")):
+            together(gated.at[2, :, chunk], c_send.at[0], c_recv.at[chunk, 4]).wait_recv()
+            for column in (0, 1):
                 for p in (0, 1):
-                    ring(chunk, name, p).wait_recv()
                     pair(chunk, 2, p, column).start()
 
     def arrived_pairs(chunk, slot):
         if slot == 0:
-            together(gated.at[0, 1, chunk], s_send.at[0], s_recv.at[chunk, 0, 0]).wait_recv()
+            together(gated.at[0, 1, chunk], s_send.at[0], s_recv.at[chunk, 0]).wait_recv()
         elif slot == 2:
 
             @pl.when(first_core)
             def _():
-                together(gated.at[2, :, chunk], s_send.at[0], s_recv.at[chunk, 0, 2]).wait_recv()
+                together(gated.at[2, :, chunk], s_send.at[0], s_recv.at[chunk, 1]).wait_recv()
 
         else:
             ahead = 0 if slot == 1 else 1
@@ -368,21 +368,23 @@
 
             pair(chunk, slot, 1 - ahead).wait_recv()
 
-    def project(chunk, slot, first=False, last=False):
-        arrived_pairs(chunk, slot)
-        if chunk == 0 and slot == 0:
-            loads[14].wait()
-        y_from = lax.rem(y_me + SIDE - slot, SIDE)
-        width = LANES // 2
-        right = []
-        for c in (core, 1 - core):
-            start = pl.multiple_of((2 * y_from + c) * CH + chunk * width, width)
-            right += [v_weight[pl.ds(start, width), :]] * 2
-        left = jnp.concatenate([gated[slot, 0, chunk], gated[slot, 1, chunk]], axis=1)
-        upper = lane_bit(left.shape, width)
+    def project(items, first=False, last=False):
+        lefts, rights = [], []
+        for chunk, slot in items:
+            arrived_pairs(chunk, slot)
+            if chunk == 0 and slot == 0:
+                loads[14].wait()
+            y_from = lax.rem(y_me + SIDE - slot, SIDE)
+            width = LANES // 2
+            for c in (core, 1 - core):
+                start = pl.multiple_of((2 * y_from + c) * CH + chunk * width, width)
+                rights += [v_weight[pl.ds(start, width), :]] * 2
+            lefts += [gated[slot, 0, chunk], gated[slot, 1, chunk]]
+        left = jnp.concatenate(lefts, axis=1)
+        upper = lane_bit(left.shape, LANES // 2)
         none = jnp.zeros_like(left)
         left = jnp.concatenate([jnp.where(upper, none, left), jnp.where(upper, left, none)], axis=0)
-        term = dot(left, jnp.concatenate(right, axis=0))
+        term = dot(left, jnp.concatenate(rights, axis=0))
         if not first:
             term = acc[...] + term
         if last:
@@ -399,41 +401,30 @@
         convolve(chunk)
     for chunk in range(SUBS):
         gate(chunk)
-    for chunk in range(SUBS):
-        all_of(recv, chunk, a_send, a_recv).wait_send()
+    together(recv.at[:, pl.ds(0, CTX - 1)], a_send.at[0], s_recv.at[0, 0]).wait_send()
     near(0)
-    for chunk in range(SUBS):
-        all_of(y_recv, chunk, b_send, b_recv).wait_send()
+    together(y_recv.at[:, pl.ds(0, CTX - 1)], b_send.at[0], s_recv.at[0, 0]).wait_send()
     near(1)
     near(2)
     cross(0)
-    project(0, 0, first=True)
+    project([(0, 0)], first=True)
     near(3)
     cross(1)
-    project(1, 0)
+    project([(1, 0)])
     cross(2)
     far(0)
-    project(2, 0)
-    project(0, 1)
-    project(0, 3)
+    project([(2, 0), (0, 1), (0, 3)])
     cross(3)
     far(1)
-    project(3, 0)
-    project(1, 1)
-    project(1, 3)
+    project([(3, 0), (1, 1), (1, 3)])
     far(2)
-    project(0, 2)
-    project(2, 1)
-    project(2, 3)
+    project([(0, 2), (2, 1), (2, 3)])
     far(3)
-    project(1, 2)
-    project(3, 1)
-    project(3, 3)
-    project(2, 2)
-    project(3, 2, last=True)
+    project([(1, 2), (3, 1), (3, 3)])
+    project([(2, 2), (3, 2)], last=True)
 
     def sent(ref, send_sem):
-        together(ref, send_sem, s_recv.at[0, 0, 0]).wait_send()
+        together(ref, send_sem, s_recv.at[0, 0]).wait_send()
 
     sent(gated.at[0], c_send.at[0])
     sent(gated.at[0, 0], s_send.at[0])
@@ -474,14 +465,14 @@
             vmem((SIDE, 2, SUBS, HALF, LANES), BF16),
             vmem((TOK, FEATURES), F32),
             dma((15,)),
+            dma((1,)),
             dma((SUBS,)),
-            dma((SUBS,)),
-            dma((SUBS,)),
+            dma((1,)),
             dma((SUBS,)),
             dma((2,)),
-            dma((SUBS, 4, 2)),
+            dma((SUBS, 5)),
             dma((3,)),
-            dma((SUBS, 3, SIDE)),
+            dma((SUBS, 6)),
         ],
         compiler_params=pltpu.CompilerParams(
             collective_id=0, has_side_effects=True, vmem_limit_bytes=48 * 1024 * 1024

time: 34 us -> 33.6 us (0.988)
  Pallas kernels: 33.2 us -> 32.8 us
    pallas_call x1, Pallas kernels: 33.2 us -> 32.8 us  [on_device(): pl.pallas_call(kernel, out_shape=jax.ShapeDtypeStruct((TOK, FEATURES), BF...]
where the time goes in v6:
time: 33.6 us; the launch traced here: 33.5 us
  Pallas kernels  32.8 us (98%)
  local copies, waits for them, and re-layouts  0.71 us (2%)
    pallas_call x1, Pallas kernels, on_device(): pl.pallas_call(kernel, out_shape=jax.ShapeDtypeStruct((TOK, FEATURES), BF...  32.8 us
    unnamed x1, local copies, waits for them, and re-layouts  0.71 us

profile of v6, /device:TPU:1, one launch (start us, length us, event | category | flops | bytes accessed | tf_op | source)
XLA Modules:
  0.0 33.5 jit_solution(14905487975535335438)
XLA Ops:
  0.0 32.8 %hyena.1 = bf16[512,256]{1,0:T(8,128)(2,1)S(1)} custom-call(bf16[512,256]{1,0:T(8,128)(2,1)} %inner.1, bf16[512,256]{1,0:T(8,128)(2,1)} %outer.1, bf16[512,256]{1,0:T(8,128)(2,1)} %source.1, f32[512,256]{1,0:T(8,128)} %taps.1, f32[1,256]{1,0:T(1,128)} %bitcast.1, bf16[2048,2048]{1,0:T(8,128)(2,1)} %weight.1, bf16[512,512]{1,0:T(8,128)(2,1)} %constant.12.clone.row_f, ...), custom_call_target="tpu_custom_call" | custom-call | flops 3000000000 | bytes 8000000 | tf_op jit(solution)/shard_map/hyena/pallas_call | solution.py:444
  32.8 0.7 %copy.14 = bf16[512,256]{1,0:T(8,128)(2,1)} copy(bf16[512,256]{1,0:T(8,128)(2,1)S(1)} %hyena.1) | data formatting | bytes 524288

commit v7 on v6

--- a/solution.py
+++ b/solution.py
@@ -274,7 +274,7 @@
             src_ref=piece(gated.at[frm, column, chunk], p),
             dst_ref=piece(gated.at[slot, column, chunk], p),
             send_sem=c_send.at[index // 2],
-            recv_sem=c_recv.at[chunk, 4 if index >= 2 else 2 * index + p],
+            recv_sem=c_recv.at[chunk, 3 if index >= 2 else 2 * index if p == index else 1],
             device_id=(me, device),
             device_id_type=MESH,
         )
@@ -331,8 +331,8 @@
             def _(p=p):
                 ring(chunk, "far", p).start()
 
-        for name, slot, p in (("up", 1, 1), ("down", 3, 0)):
-            ring(chunk, name, p).wait_recv()
+        together(gated.at[1, 0, chunk], c_send.at[0], c_recv.at[chunk, 1]).wait_recv()
+        for slot, p in ((1, 1), (3, 0)):
             pair(chunk, slot, p).start()
 
     def cross(chunk):
@@ -345,7 +345,7 @@
     def far(chunk):
         @pl.when(second_core)
         def _():
-            together(gated.at[2, :, chunk], c_send.at[0], c_recv.at[chunk, 4]).wait_recv()
+            together(gated.at[2, :, chunk], c_send.at[0], c_recv.at[chunk, 3]).wait_recv()
             for column in (0, 1):
                 for p in (0, 1):
                     pair(chunk, 2, p, column).start()
@@ -470,7 +470,7 @@
             dma((1,)),
             dma((SUBS,)),
             dma((2,)),
-            dma((SUBS, 5)),
+            dma((SUBS, 4)),
             dma((3,)),
             dma((SUBS, 6)),
         ],

time: 33.6 us -> 33.6 us (level)
  no operation moved by 1% of the time
where the time goes in v7:
time: 33.6 us; the launch traced here: 33.5 us
  Pallas kernels  32.8 us (98%)
  local copies, waits for them, and re-layouts  0.71 us (2%)
    pallas_call x1, Pallas kernels, on_device(): pl.pallas_call(kernel, out_shape=jax.ShapeDtypeStruct((TOK, FEATURES), BF...  32.8 us
    unnamed x1, local copies, waits for them, and re-layouts  0.71 us

profile of v7, /device:TPU:1, one launch (start us, length us, event | category | flops | bytes accessed | tf_op | source)
XLA Modules:
  0.0 33.5 jit_solution(14838096457540204648)
XLA Ops:
  0.0 32.8 %hyena.1 = bf16[512,256]{1,0:T(8,128)(2,1)S(1)} custom-call(bf16[512,256]{1,0:T(8,128)(2,1)} %inner.1, bf16[512,256]{1,0:T(8,128)(2,1)} %outer.1, bf16[512,256]{1,0:T(8,128)(2,1)} %source.1, f32[512,256]{1,0:T(8,128)} %taps.1, f32[1,256]{1,0:T(1,128)} %bitcast.1, bf16[2048,2048]{1,0:T(8,128)(2,1)} %weight.1, bf16[512,512]{1,0:T(8,128)(2,1)} %constant.12.clone.row_f, ...), custom_call_target="tpu_custom_call" | custom-call | flops 3000000000 | bytes 8000000 | tf_op jit(solution)/shard_map/hyena/pallas_call | solution.py:444
  32.8 0.7 %copy.14 = bf16[512,256]{1,0:T(8,128)(2,1)} copy(bf16[512,256]{1,0:T(8,128)(2,1)S(1)} %hyena.1) | data formatting | bytes 524288
